TPU v7x, 256 devices: a whole 4x4x8 slice. The times are simulated.
256 devices in a mesh: mp: 2 (over x_lo), tok: 16 (over z, core), vocab: 8 (over x_hi, y).
Axes of the slice: x: 4 (x_hi: 2, x_lo: 2; x = x_hi * 2 + x_lo), y: 4, z: 8, core: 2. Of those that a mesh axis runs over, the one named last changes fastest.
Arguments:
- hidden: bfloat16 [2, 128, 5120], P('mp', 'tok'), may hold values from -400 to 400
- norm_gain: float32 [2, 5120], P('mp'), may hold values from 0.5 to 1.5
- output_head: bfloat16 [2, 76800, 5120], P('mp', 'vocab', 'tok'), may hold values from -0.703125 to 0.703125
- token_ids: int32 [128], P('tok'), may hold values from 0 to 76799
- live_mask: int32 [128], P('tok'), may hold values from 0 to 1, as said below
- advantages: float32 [128], P('tok'), may hold values from -4 to 4
Outputs:
- hidden_grad: float32 [128, 5120], P('tok', 'mp')
- head_grad: bfloat16 [2, 38400, 5120], P('mp', 'vocab', 'tok')
Inputs may be any that keep to these rules, and one draw needn't show every extreme that they name: `live_mask`: 1 marks a response token, 0 a masked one; the last token is live.
All inputs are finite; a program needn't handle non-finite values.
Results may differ from a plain program's by a relative error of at most 0.0044.
The roundings to bfloat16 on the way count: a program that leaves them out, or rounds other values in their place, can miss the bound.
Values may be sent and summed in bfloat16 or wider, within the bound.
A program may use at most 64 MiB of HBM per device.

v0:
```python
import jax
import jax.numpy as jnp
from jax import lax
from jax.sharding import PartitionSpec as P

loss_scale = 256.0
kl_coef = 0.1
norm_eps = 1e-06


def passed_along(value, axis, steps):
    count = lax.axis_size(axis)
    initial, last = (max(0, -steps), min(count, count - steps))
    return lax.ppermute(value, axis, [(source, source + steps) for source in range(initial, last)])


def joined(part, axis, combine):
    gathered = jax.tree.map(lambda a: lax.all_gather(a, axis), part)

    def take(source):
        return jax.tree.map(lambda a: lax.dynamic_index_in_dim(a, source, 0, False), gathered)

    return lax.fori_loop(
        1, lax.axis_size(axis), lambda source, state: combine(state, take(source)), take(0)
    )


def partner(block, axis, distance):
    count = lax.axis_size(axis)
    route = []
    for low in range(count):
        high = low | 1 << distance
        if high != low and high < count:
            route += [(low, high), (high, low)]
    return lax.ppermute(block, axis, route)


def combine_stats(left_pair, right_pair):
    row_high = jnp.maximum(left_pair[0], right_pair[0])
    row_total = left_pair[1] * jnp.exp(left_pair[0] - row_high) + right_pair[1] * jnp.exp(
        right_pair[0] - row_high
    )
    return (row_high, row_total)


def token_grad(policy_prob, lp_diff, kl_part, onehot, token_coef, advantage):
    inner = advantage * (policy_prob - onehot) + kl_coef * policy_prob * (lp_diff - kl_part)
    return (token_coef * inner).astype(jnp.bfloat16)


def per_device(hidden, norm_gain, output_head, token_ids, live_mask, advantages):
    model_index = lax.axis_index("mp")
    token_block = lax.axis_index("tok")
    vocab_block = lax.axis_index("vocab")
    values = hidden[0].astype(jnp.float32)
    inv_rms = lax.rsqrt(jnp.mean(values * values, axis=1, keepdims=True) + norm_eps)
    unit_rows = values * inv_rms
    normed = (unit_rows * norm_gain[0]).astype(jnp.bfloat16)
    columns = lax.all_to_all(normed, "tok", split_axis=1, concat_axis=0, tiled=True)
    weights = output_head[0]
    vocab_dev = weights.shape[0]
    half_rows = vocab_dev // 2
    shifted = passed_along(columns, "mp", 1)
    dw_source = jnp.where(model_index == 0, columns, shifted)
    live_f = live_mask.astype(jnp.float32)
    contract = (((1,), (1,)), ((), ()))
    lead_contract = (((0,), (0,)), ((), ()))
    slab_rows = vocab_dev // lax.axis_size("tok")
    logits = lax.psum_scatter(
        lax.dot_general(weights, columns, contract, preferred_element_type=jnp.float32),
        "tok",
        scatter_dimension=0,
        tiled=True,
    )
    local_high = jnp.max(logits, axis=0)
    local_total = jnp.sum(jnp.exp(logits - local_high[None, :]), axis=0)
    row_high, row_total = joined((local_high, local_total), ("tok", "vocab"), combine_stats)
    own_lp = logits - (row_high + jnp.log(row_total))[None, :]
    peer_lp = partner(own_lp, "mp", 0)
    policy_lp = jnp.where(model_index == 0, own_lp, peer_lp)
    ref_lp = jnp.where(model_index == 0, peer_lp, own_lp)
    lp_diff = policy_lp - ref_lp
    policy_prob = jnp.exp(policy_lp)
    ids_all = lax.all_gather(token_ids, "tok", axis=0, tiled=True)
    token_meta = lax.all_gather(jnp.stack([live_f, advantages]), "tok", axis=1, tiled=True)
    live_total = jnp.sum(token_meta[0])
    kl_sum = lax.psum(jnp.sum(policy_prob * lp_diff, axis=0), ("tok", "vocab"))
    entry_index = (
        vocab_block * vocab_dev
        + token_block * slab_rows
        + lax.broadcasted_iota(jnp.int32, (slab_rows, 1), 0)
    )
    onehot = (entry_index == ids_all[None, :]).astype(jnp.float32)
    token_coef = (loss_scale * token_meta[0] / live_total)[None, :]
    logit_grad = token_grad(
        policy_prob, lp_diff, kl_sum[None, :], onehot, token_coef, token_meta[1][None, :]
    )
    all_grad = lax.all_gather(logit_grad, "tok", axis=0, tiled=True)
    feature_grad = lax.dot_general(
        all_grad, weights, lead_contract, preferred_element_type=jnp.float32
    )
    half_grad = lax.dynamic_slice_in_dim(all_grad, model_index * half_rows, half_rows, 0)
    head_part = jnp.dot(half_grad, dw_source, preferred_element_type=jnp.float32)
    summed = lax.psum(feature_grad, "vocab")
    row_grad = lax.all_to_all(summed, "tok", split_axis=0, concat_axis=1, tiled=True)
    scaled = row_grad * norm_gain[0]
    full_grad = inv_rms * (scaled - unit_rows * jnp.mean(unit_rows * scaled, axis=1, keepdims=True))
    width_half = full_grad.shape[1] // 2
    moved_cols = passed_along(full_grad[:, width_half:], "mp", 1)
    hidden_grad = jnp.where(model_index == 0, full_grad[:, :width_half], moved_cols)
    return (hidden_grad, head_part.astype(jnp.bfloat16)[None])


def solution(mesh):
    placed = (
        P("mp", "tok", None),
        P("mp", None),
        P("mp", "vocab", "tok"),
        P("tok"),
        P("tok"),
        P("tok"),
    )
    return jax.shard_map(
        per_device,
        mesh=mesh,
        in_specs=placed,
        out_specs=(P("tok", "mp"), P("mp", "vocab", "tok")),
        check_vma=False,
    )
```

profile of v0, /device:TPU:2, one launch (start us, length us, event | category | flops | bytes accessed | tf_op | source)
XLA Modules:
  0.0 1304.4 jit_solution(13124511290509388310)
XLA Ops:
  7.2 1.0 fusion.12
  8.3 1.0 reshape.47
  9.8 1.4 reduce.4
  11.4 16.7 %all_to_all.35 = bf16[8,16,320]{2,0,1:T(8,128)(2,1)S(1)} all-to-all(bf16[8,16,320]{2,0,1:T(8,128)(2,1)S(1)} %fusion.11), channel_id=1, replica_groups=mesh['mp'=2,'tok'=16,'vocab'=8] {'tok'}, dimensions={1} | all-to-all | bytes 163840 | tf_op jit(solution)/shard_map/all_to_all | solution.py:59
  28.1 6.4 convolution_bitcast_fusion
  35.2 14.8 %all-gather.2 = f32[16,8,2]{1,2,0:T(2,128)S(1)} all-gather(f32[1,8,2]{1,2,0:T(2,128)S(1)} %maximum_bitcast_fusion), channel_id=1, replica_groups=mesh['mp'=2,'tok'=16,'vocab'=8] {'tok'}, dimensions={0}, use_global_device_ids=true | all-gather | bytes 1088 | tf_op jit(solution)/shard_map/all_gather | solution.py:85
  52.3 11.8 all-reduce
  64.1 91.6 %all-reduce.7.cloned.1.call-done = f32[9600,128]{0,1:T(8,128)} async-done(((f32[9600,128]{0,1:T(8,128)}), f32[9600,128]{0,1:T(8,128)}) %all-reduce.7.cloned.1.call-update) | async-done | bytes 4915216
  155.7 1.2 dynamic-slice_reduce_fusion
  156.9 1.3 exponential_reduce_fusion
  158.2 324.2 %all-gather.4 = f32[128,1,128]{2,1,0:T(1,128)S(1)} all-gather(f32[1,1,128]{2,1,0:T(1,128)S(1)} %bitcast.83), channel_id=3, replica_groups=mesh['mp'=2,'tok'=16,'vocab'=8] {'tok','vocab'}, dimensions={0}, use_global_device_ids=true | all-gather | bytes 66048 | tf_op jit(solution)/shard_map/all_gather | solution.py:18
  482.4 317.8 %all-gather.3 = f32[128,1,128]{2,1,0:T(1,128)S(1)} all-gather(f32[1,1,128]{2,1,0:T(1,128)S(1)} %bitcast.80), channel_id=2, replica_groups=mesh['mp'=2,'tok'=16,'vocab'=8] {'tok','vocab'}, dimensions={0}, use_global_device_ids=true | all-gather | bytes 66048 | tf_op jit(solution)/shard_map/all_gather | solution.py:18
  800.2 5.7 while.17
  806.0 1.2 dynamic-slice_subtract_fusion
  807.2 1.5 collective-permute-start
  808.7 0.6 slice_reduce_fusion
  809.3 0.6 divide_bitcast_fusion
  809.9 4.4 collective-permute-done
  814.4 1.3 multiply_reduce_fusion
  815.6 325.9 %psum.14 = f32[128]{0:T(128)S(1)} all-reduce(f32[128]{0:T(128)S(1)} %multiply_reduce_fusion), channel_id=1, replica_groups=mesh['mp'=2,'tok'=16,'vocab'=8] {'tok','vocab'}, use_global_device_ids=true, to_apply=%region_8.9 | all-reduce | flops 128 | bytes 1024 | tf_op jit(solution)/shard_map/psum | solution.py:87
  1141.5 1.3 multiply_convert_fusion
  1142.8 0.8 copy.18
  1143.7 35.1 %all-gather.7.cloned.1.call-done = bf16[9600,128]{1,0:T(8,128)(2,1)} async-done(((bf16[600,128]{1,0:T(8,128)(2,1)}), bf16[9600,128]{1,0:T(8,128)(2,1)}) %all-gather.7.cloned.1.call-update) | async-done | bytes 2457616 | tf_op jit(solution)/shard_map/all_gather | solution.py:98
  1178.8 6.6 fusion.7
  1185.4 87.2 %all-reduce.5.cloned.1.call-done = f32[16,8,320]{2,1,0:T(8,128)} async-done(((f32[16,8,320]{2,1,0:T(8,128)}), f32[16,8,320]{2,1,0:T(8,128)}) %all-reduce.5.cloned.1.call-update) | async-done | bytes 163856 | tf_op jit(solution)/shard_map/psum | solution.py:104
  1272.6 7.1 all-to-all-start.1
  1279.7 1.3 collective-permute-start.2
  1281.0 8.6 all-to-all-done.1
  1290.2 1.3 collective-permute-start.1
  1291.5 2.7 fusion.2
  1294.2 3.0 collective-permute-done.1
  1297.2 0.6 slice_select_fusion
  (169 shorter events, 6.4 us)
Async XLA Ops:
  7.2 148.6 %all-reduce.7.cloned.1.call-start = ((), (), s32[]{:S(2)}) async-start(), calls=%async_computation.4 | async-start | bytes 9830400
  34.5 0.7 copy-start.5
  34.5 0.7 copy-start.4
  34.5 15.6 %copy-start.3 = (u32[256]{0:T(256)S(1)}, u32[256]{0:T(256)}, u32[]{:S(2)}) copy-start(u32[256]{0:T(256)} %constant.89) | copy-start | bytes 3076
  34.5 17.5 %copy-start.6 = (s32[8]{0:T(128)S(1)}, s32[8]{0:T(128)}, u32[]{:S(2)}) copy-start(s32[8]{0:T(128)} %param.11) | copy-start | bytes 100
  34.5 1144.3 %all-gather.7.cloned.1.call-start = ((), (), s32[]{:S(2)}) async-start(), calls=%async_computation.2 | async-start | bytes 2611200 | tf_op jit(solution)/shard_map/all_gather | solution.py:98
  807.2 7.2 collective-permute-start
  1143.7 146.2 %copy-start.1 = (bf16[1,8,5120]{2,1,0:T(8,128)(2,1)S(1)}, bf16[1,8,5120]{2,1,0:T(8,128)(2,1)}, u32[]{:S(2)}) copy-start(bf16[1,8,5120]{2,1,0:T(8,128)(2,1)} %param.8) | copy-start | bytes 245764
  1143.7 146.2 %copy-start.2 = (f32[1,5120]{1,0:T(1,128)S(1)}, f32[1,5120]{1,0:T(1,128)}, u32[]{:S(2)}) copy-start(f32[1,5120]{1,0:T(1,128)} %param.9) | copy-start | bytes 61444
  1143.7 128.9 %all-reduce.5.cloned.1.call-start = ((), (), s32[]{:S(2)}) async-start(), calls=%async_computation.3 | async-start | bytes 393216 | tf_op jit(solution)/shard_map/psum | solution.py:104
  1178.8 112.7 %copy-start = (bf16[9600,128]{1,0:T(8,128)(2,1)S(1)}, bf16[9600,128]{1,0:T(8,128)(2,1)}, u32[]{:S(2)}) copy-start(bf16[9600,128]{1,0:T(8,128)(2,1)} %all-gather.7.cloned.1.call-done) | copy-start | bytes 7372804
  1272.6 17.1 %all-to-all-start.1 = ((f32[16,8,320]{2,1,0:T(8,128)}), f32[16,8,320]{2,1,0:T(8,128)S(1)}, u32[]{:S(2)}, u32[]{:S(2)}) async-start(f32[16,8,320]{2,1,0:T(8,128)} %all-reduce.5.cloned.1.call-done), calls=%async_computation.1 | async-start | bytes 393216 | tf_op jit(solution)/shard_map/all_to_all | solution.py:105
  1279.7 11.8 collective-permute-start.2
  1290.2 7.0 collective-permute-start.1
Sparse Core Ops, SparseCore 0:
  34.6 121.0 all-reduce.6
  1143.8 34.9 all-gather.6
  1185.5 87.0 all-reduce.4
where the time goes:
time: 1310 us; the launch traced here: 1300 us
  blocking collectives  1010 us (77%)
  waiting for transfers between devices  230 us (18%)
  matrix products  15.7 us (1%)
  between operations  15.3 us (1%)
  other arithmetic  14.5 us (1%)
    all_gather x2, blocking collectives, joined(): gathered = jax.tree.map(lambda a: lax.all_gather(a, axis), part)  642 us
    psum x1, blocking collectives, per_device(): kl_sum = lax.psum(jnp.sum(policy_prob * lp_diff, axis=0), ('tok', 'vocab'))  326 us
    unnamed x4, waiting for transfers between devices  91.7 us
    psum x1, waiting for transfers between devices, per_device(): summed = lax.psum(feature_grad, 'vocab')  87.2 us
    all_gather x1, waiting for transfers between devices, per_device(): all_grad = lax.all_gather(logit_grad, 'tok', axis=0, tiled=True)  35.1 us
  transfers between devices with their start and end apart: 7, of which 6 were waited for; matrix products, arithmetic and copies ran while one was open for 0% of the time, Pallas kernels for 0%

commit v1 on v0

v1 whole, which is shorter than its diff:
```python
import functools

import jax
import jax.numpy as jnp
from jax import lax
from jax.experimental import pallas as pl
from jax.experimental.pallas import tpu as pltpu
from jax.sharding import PartitionSpec as P

loss_scale = 256.0
kl_coef = 0.1
norm_eps = 1e-06
MESH = pl.DeviceIdType.MESH
f32 = jnp.float32
bf16 = jnp.bfloat16


class Sems:
    def __init__(self):
        self.count = 0

    def take(self, number):
        first = self.count
        self.count += number
        return first


def sem_plan(nt, nz, nv):
    sems = Sems()
    half = nz // 2
    ring = 2 + 4 * (half - 1)
    plan = dict(
        a2a=sems.take(nt), meta=sems.take(nt), dw=sems.take(1), unit=sems.take(1), inv=sems.take(1),
        pair=sems.take(nz), up=sems.take(ring), down=sems.take(ring), peer=sems.take(4),
        tstat=sems.take(nt), vstat=sems.take(nv),
        gup=sems.take(2 * half - 1), gdown=sems.take(2 * half - 1), gpair=sems.take(2 * nz),
        fa=sems.take(nt), fr=sems.take(nv), fb=sems.take(2 * nv),
    )
    return plan, sems.count


def kernel(nt, nz, nv, plan, n_sem,
           hidden, gain, head, ids, live, adv,
           hg_out, head_out,
           wbuf, lbuf, xbuf, rbuf, ybuf, gbuf, hbuf,
           nbuf, cbuf, ubuf, urecv, ibuf, irecv, gainb, mbuf, colb, dwb,
           tst, vst, fbuf, fabuf, frbuf, fbb,
           wsem, hsem, ss, rs):
    mp = lax.axis_index("mp")
    tok = lax.axis_index("tok")
    voc = lax.axis_index("vocab")
    zi = tok // 2
    core = tok % 2
    sib = tok + 1 - 2 * core
    half = nz // 2
    T = nt * 8
    chip_rows = wbuf.shape[1]
    width = wbuf.shape[2]
    R = xbuf.shape[1]
    off = chip_rows - R
    over = R - off
    Q = R // 4
    H2 = R // 2
    spv = nt // nv
    pending = []

    def rcopy(src, dst, name, index, dev):
        at = plan[name] + index
        return pltpu.make_async_remote_copy(
            src_ref=src, dst_ref=dst, send_sem=ss.at[at], recv_sem=rs.at[at],
            device_id=dev, device_id_type=MESH)

    def zat(o):
        return lax.rem(zi + o + nz, nz)

    def up_dev():
        return {"tok": lax.rem(tok + 2, nt)}

    def down_dev():
        return {"tok": lax.rem(tok + nt - 2, nt)}

    def sib_dev():
        return {"tok": sib}

    order = [half]
    for d in range(half - 1, 0, -1):
        order += [d, -d]
    order += [0]

    def wcopy(k):
        z = zat(order[k])
        return pltpu.make_async_copy(
            head.at[0, pl.ds(pl.multiple_of(z * chip_rows, 16), chip_rows), :], wbuf.at[z], wsem.at[k])

    for k in range(nz):
        wcopy(k).start()

    barrier = pltpu.get_barrier_semaphore()

    @pl.loop(1, nt)
    def _(j):
        pl.semaphore_signal(barrier, inc=1, device_id={"tok": lax.rem(tok + j, nt)}, device_id_type=MESH)

    @pl.loop(1, nv)
    def _(j):
        pl.semaphore_signal(barrier, inc=1, device_id={"vocab": lax.rem(voc + j, nv)}, device_id_type=MESH)

    @pl.loop(0, nv)
    def _(j):
        pl.semaphore_signal(
            barrier, inc=1, device_id={"mp": 1 - mp, "vocab": lax.rem(voc + j, nv)}, device_id_type=MESH)

    x = hidden[0].astype(f32)
    inv = lax.rsqrt(jnp.mean(x * x, axis=1, keepdims=True) + norm_eps)
    unit = x * inv
    g = gain[...]
    normed = (unit * g).astype(bf16).astype(f32)
    for k in range(nt):
        cols = slice(k * width, (k + 1) * width)
        nbuf[k] = normed[:, cols]
        ubuf[k] = unit[:, cols]
        gainb[k] = jnp.broadcast_to(g[:, cols], (8, width))
    ibuf[...] = jnp.broadcast_to(inv, ibuf.shape)

    lane = lax.broadcasted_iota(jnp.int32, (8, T), 1)
    row = lax.broadcasted_iota(jnp.int32, (8, T), 0)
    id_row = jnp.zeros((8, T), jnp.int32)
    live_row = jnp.zeros((8, T), jnp.int32)
    adv_row = jnp.zeros((8, T), f32)
    for j in range(8):
        here = lane == tok * 8 + j
        id_row = jnp.where(here, ids[j], id_row)
        live_row = jnp.where(here, live[j], live_row)
        adv_row = jnp.where(here, adv[j], adv_row)
    mbuf[tok] = jnp.where(row == 0, id_row.astype(f32), jnp.where(row == 1, live_row.astype(f32), adv_row))
    cbuf[tok] = nbuf[tok]

    pl.semaphore_wait(barrier, nt - 1 + nv - 1 + nv)

    def a2a_copy(j):
        p = lax.rem(tok + j, nt)
        return rcopy(nbuf.at[p], cbuf.at[tok], "a2a", j, {"tok": p})

    def meta_copy(j):
        p = lax.rem(tok + j, nt)
        return rcopy(mbuf.at[tok], mbuf.at[tok], "meta", j, {"tok": p})

    @pl.loop(1, nt)
    def _(j):
        a2a_copy(j).start()

    @pl.loop(1, nt)
    def _(j):
        a2a_copy(j).wait_recv()

    colb[...] = cbuf[...].reshape(T, width).astype(bf16)

    def logits(k):
        z = zat(order[k])
        wcopy(k).wait()
        lbuf[z] = lax.dot_general(
            wbuf[z], colb[...], (((1,), (1,)), ((), ())), preferred_element_type=f32)
        other = pl.multiple_of((1 - core) * off, 8)
        c = rcopy(lbuf.at[z, pl.ds(other, R), :], xbuf.at[z], "pair", k, sib_dev())
        c.start()
        pending.append(c)
        return c

    def pair_add(k, c):
        z = zat(order[k])
        c.wait_recv()
        xbuf[z] = xbuf[z] + lbuf[z, pl.ds(pl.multiple_of(core * off, 8), R), :]

    def ring_list(first_pieces, rest):
        out = [(half, q) for q in first_pieces]
        for d in range(half - 1, 0, -1):
            out += [(d, q) for q in rest(d)]
        return out

    up_list = ring_list((0, 1), lambda d: (2, 3, 0, 1))
    down_list = ring_list((2, 3), lambda d: (2, 3, 0, 1) if d < 3 else (0, 1, 2, 3))
    slot = {}
    for i, m in enumerate(up_list):
        slot[("up",) + m] = i
    for i, m in enumerate(down_list):
        slot[("down",) + m] = i
    ring_len = len(up_list)

    def ring_copy(way, d, q):
        z = zat(d if way == "up" else -d)
        i = slot[(way, d, q)]
        return rcopy(
            xbuf.at[z, pl.ds(q * Q, Q), :], rbuf.at[i if way == "up" else ring_len + i], way, i,
            up_dev() if way == "up" else down_dev())

    def ring_send(way, d, q):
        c = ring_copy(way, d, q)
        c.start()
        pending.append(c)

    def has(way, d, q):
        return (way, d, q) in slot

    def arrived(way, d, q):
        ring_copy(way, d, q).wait_recv()
        i = slot[(way, d, q)]
        return rbuf[i if way == "up" else ring_len + i]

    ready = []
    for k in range(nz):
        ready.append(logits(k))
        if k >= 1:
            pair_add(k - 1, ready[k - 1])
            o = order[k - 1]
            if o == half:
                for q in (0, 1):
                    ring_send("up", half, q)
                    ring_send("down", half, q + 2)
            elif o == half - 1 and o > 0:
                for q in (2, 3):
                    ring_send("up", o, q)
            elif o == -(half - 1) and o < 0:
                for q in (0, 1):
                    ring_send("down", -o, q)
    pair_add(nz - 1, ready[nz - 1])

    dw_copy = rcopy(colb, dwb, "dw", 0, {"mp": 1 - mp})
    unit_copy = rcopy(ubuf.at[pl.ds(nt // 2, nt // 2)], urecv, "unit", 0, {"mp": 1 - mp})
    inv_copy = rcopy(ibuf, irecv, "inv", 0, {"mp": 1 - mp})
    for c in (dw_copy, unit_copy, inv_copy):
        c.start()
        pending.append(c)

    @pl.loop(1, nt)
    def _(j):
        meta_copy(j).start()

    def step(way, d, q):
        r = arrived(way, d, q)
        z = zat(d - 1 if way == "up" else 1 - d)
        rows = pl.ds(q * Q, Q)
        xbuf[z, rows, :] = xbuf[z, rows, :] + r
        if d > 1:
            ring_send(way, d - 1, q)

    def peer_copy(q):
        return rcopy(xbuf.at[zi, pl.ds(q * Q, Q), :], ybuf.at[pl.ds(q * Q, Q), :], "peer", q, {"mp": 1 - mp})

    for mu, md in zip(up_list, down_list):
        step("up", *mu)
        step("down", *md)
        if mu[0] == 1:
            c = peer_copy(mu[1])
            c.start()
            pending.append(c)

    @pl.loop(1, nt)
    def _(j):
        meta_copy(j).wait_recv()

    meta = jnp.sum(mbuf[...], axis=0)
    id_all = meta[0:1].astype(jnp.int32)
    live_all = meta[1:2]
    adv_all = meta[2:3]
    coef = loss_scale * live_all / jnp.sum(live_all)

    for q in (2, 3, 0, 1):
        peer_copy(q).wait_recv()

    own = xbuf[zi]
    peer = ybuf[...]
    l0 = jnp.where(mp == 0, own, peer)
    l1 = jnp.where(mp == 0, peer, own)
    rid = lax.broadcasted_iota(jnp.int32, (R, 1), 0)
    counted = jnp.where((rid >= over) | (core == 0), 1.0, 0.0).astype(f32)

    def tile_of(rows):
        out = jnp.zeros((8, T), f32)
        for i, r in enumerate(rows):
            out = jnp.where(row == i, r, out)
        return out

    h0 = jnp.max(l0, axis=0, keepdims=True)
    h1 = jnp.max(l1, axis=0, keepdims=True)
    e0 = jnp.exp(l0 - h0) * counted
    e1 = jnp.exp(l1 - h1) * counted
    tst[tok] = tile_of([
        h0, jnp.sum(e0, axis=0, keepdims=True), jnp.sum(e0 * (l0 - l1), axis=0, keepdims=True),
        h1, jnp.sum(e1, axis=0, keepdims=True)])

    def tstat_copy(j):
        return rcopy(tst.at[tok], tst.at[tok], "tstat", j, {"tok": lax.rem(tok + j, nt)})

    def vstat_copy(j):
        return rcopy(vst.at[voc], vst.at[voc], "vstat", j, {"vocab": lax.rem(voc + j, nv)})

    def combined(b):
        s = b[...]
        m0, s0, t0, m1, s1 = (s[:, i, :] for i in range(5))
        h0 = jnp.max(m0, axis=0, keepdims=True)
        h1 = jnp.max(m1, axis=0, keepdims=True)
        w0 = jnp.exp(m0 - h0)
        w1 = jnp.exp(m1 - h1)
        return [h0, jnp.sum(s0 * w0, axis=0, keepdims=True), jnp.sum(t0 * w0, axis=0, keepdims=True),
                h1, jnp.sum(s1 * w1, axis=0, keepdims=True)]

    @pl.loop(1, nt)
    def _(j):
        tstat_copy(j).start()

    @pl.loop(1, nt)
    def _(j):
        tstat_copy(j).wait_recv()

    vst[voc] = tile_of(combined(tst))

    @pl.loop(1, nv)
    def _(j):
        vstat_copy(j).start()

    @pl.loop(1, nv)
    def _(j):
        vstat_copy(j).wait_recv()

    h0, s0, t0, h1, s1 = combined(vst)
    lse0 = h0 + jnp.log(s0)
    lse1 = h1 + jnp.log(s1)
    kl = t0 / s0 - (lse0 - lse1)

    lp0 = l0 - lse0
    diff = lp0 - (l1 - lse1)
    prob = jnp.exp(lp0)
    entry = voc * (nz * chip_rows) + zi * chip_rows + core * off + rid
    onehot = jnp.where(entry == id_all, 1.0, 0.0).astype(f32)
    gbuf[core, zi] = (coef * (adv_all * (prob - onehot) + kl_coef * prob * (diff - kl))).astype(bf16)

    gup = [(s, h) for s in range(1, half) for h in (0, 1)] + [(half, 0)]
    gdown = [(s, h) for s in range(1, half) for h in (0, 1)] + [(half, 1)]

    def gring(way, s, h):
        z = zat(1 - s if way == "gup" else s - 1)
        view = gbuf.at[core, z, pl.ds(h * H2, H2), :]
        return rcopy(view, view, way, (gup if way == "gup" else gdown).index((s, h)),
                     up_dev() if way == "gup" else down_dev())

    def gring_recv(way, s, h):
        z = zat(-s if way == "gup" else s)
        view = gbuf.at[core, z, pl.ds(h * H2, H2), :]
        return rcopy(view, view, way, (gup if way == "gup" else gdown).index((s, h)),
                     up_dev() if way == "gup" else down_dev())

    def gpair(o, h):
        view = gbuf.at[core, zat(o), pl.ds(h * H2, H2), :]
        return rcopy(view, view, "gpair", 2 * (o % nz) + h, sib_dev())

    def gpair_recv(o, h):
        view = gbuf.at[1 - core, zat(o), pl.ds(h * H2, H2), :]
        return rcopy(view, view, "gpair", 2 * (o % nz) + h, sib_dev())

    def begin(c):
        c.start()
        pending.append(c)

    for h in (0, 1):
        if (1, h) in gup:
            begin(gring("gup", 1, h))
        if (1, h) in gdown:
            begin(gring("gdown", 1, h))
    for h in (0, 1):
        begin(gpair(0, h))

    def feature(o):
        for h in (0, 1):
            gpair_recv(o, h).wait_recv()

        @pl.when(mp == 0)
        def _():
            z = zat(o)
            tn = (((0,), (0,)), ((), ()))
            part = lax.dot_general(
                gbuf[0, z], wbuf[z, 0:R, :], tn, preferred_element_type=f32)
            part = part + lax.dot_general(
                gbuf[1, z, over:R, :], wbuf[z, R:chip_rows, :], tn, preferred_element_type=f32)
            part = part.reshape(nt, 8, width)
            if o == 0:
                fbuf[...] = part
            else:
                fbuf[...] = fbuf[...] + part

    last = [0]
    for s in range(1, half + 1):
        now = []
        for h in (0, 1):
            for way, todo in (("gup", gup), ("gdown", gdown)):
                if (s, h) in todo:
                    gring_recv(way, s, h).wait_recv()
                    if (s + 1, h) in todo:
                        begin(gring(way, s + 1, h))
                    o = -s if way == "gup" else s
                    if s == half:
                        o = half
                    begin(gpair(o, h))
                    if o not in now:
                        now.append(o)
        for o in last:
            feature(o)
        last = now
    for o in last:
        feature(o)

    def fa_copy(j):
        p = lax.rem(tok + j, nt)
        return rcopy(fbuf.at[p], fabuf.at[tok], "fa", j, {"tok": p})

    def fr_copy(j):
        p = lax.rem(voc + j, nv)
        return rcopy(fabuf.at[pl.ds(p * spv, spv)], frbuf.at[voc], "fr", j, {"vocab": p})

    def fb_copy(j, other):
        p = lax.rem(voc + j, nv)
        return rcopy(fbb.at[voc], fbb.at[voc], "fb", other * nv + j, {"mp": other, "vocab": p})

    @pl.when(mp == 0)
    def _():
        @pl.loop(1, nt)
        def _(j):
            fa_copy(j).start()

        fabuf[tok] = fbuf[tok]

    for c in (dw_copy, unit_copy, inv_copy):
        c.wait_recv()
    dw = jnp.where(mp == 0, colb[...].astype(f32), dwb[...].astype(f32)).astype(bf16)

    def hcopy(i):
        return pltpu.make_async_copy(hbuf.at[i], head_out.at[0, pl.ds(i * chip_rows, chip_rows), :], hsem.at[i])

    def head_rows(i):
        z = mp * half + i
        hbuf[i, 0:R, :] = jnp.dot(gbuf[0, z], dw, preferred_element_type=f32).astype(bf16)
        hbuf[i, R:chip_rows, :] = jnp.dot(
            gbuf[1, z, over:R, :], dw, preferred_element_type=f32).astype(bf16)
        hcopy(i).start()

    for i in range(half // 2):
        head_rows(i)

    @pl.when(mp == 0)
    def _():
        @pl.loop(1, nt)
        def _(j):
            fa_copy(j).wait_recv()

        @pl.loop(1, nv)
        def _(j):
            fr_copy(j).start()

        frbuf[voc] = fabuf[pl.ds(voc * spv, spv)]

    for i in range(half // 2, half):
        head_rows(i)

    @pl.when(mp == 0)
    def _():
        @pl.loop(1, nv)
        def _(j):
            fr_copy(j).wait_recv()

        scaled = jnp.sum(frbuf[...], axis=0) * gainb[pl.ds(voc * spv, spv)]
        mine = ubuf[pl.ds(voc * spv, spv)] * scaled
        dot = jnp.sum(jnp.sum(mine, axis=2, keepdims=True), axis=0)
        fbb[voc, 0:spv] = scaled
        fbb[voc, spv] = jnp.broadcast_to(dot, (8, width))

        @pl.loop(1, nv)
        def _(j):
            fb_copy(j, 0).start()

        @pl.loop(0, nv)
        def _(j):
            fb_copy(j, 1).start()

        @pl.loop(1, nv)
        def _(j):
            fb_copy(j, 0).wait_recv()

    @pl.when(mp == 1)
    def _():
        @pl.loop(0, nv)
        def _(j):
            fb_copy(j, 1).wait_recv()

    mean = jnp.sum(fbb[:, spv], axis=0) * (1.0 / (nt * width))
    inv_pol = jnp.where(mp == 0, ibuf[:, 0:1], irecv[:, 0:1])
    for i in range(nt // 2):
        slab = mp * (nt // 2) + i
        unit_pol = jnp.where(mp == 0, ubuf[i], urecv[i])
        hg_out[i] = inv_pol * (fbb[slab // spv, lax.rem(slab, spv)] - unit_pol * mean)

    for i in range(half):
        hcopy(i).wait()
    for c in pending:
        c.wait_send()

    @pl.loop(1, nt)
    def _(j):
        a2a_copy(j).wait_send()
        meta_copy(j).wait_send()
        tstat_copy(j).wait_send()

    @pl.loop(1, nv)
    def _(j):
        vstat_copy(j).wait_send()

    @pl.when(mp == 0)
    def _():
        @pl.loop(1, nt)
        def _(j):
            fa_copy(j).wait_send()

        @pl.loop(1, nv)
        def _(j):
            fr_copy(j).wait_send()
            fb_copy(j, 0).wait_send()

        @pl.loop(0, nv)
        def _(j):
            fb_copy(j, 1).wait_send()


def per_device(nt, nv, hidden, norm_gain, output_head, token_ids, live_mask, advantages):
    nz = nt // 2
    half = nz // 2
    rows, width = output_head.shape[1:]
    chip_rows = rows // nz
    R = (chip_rows // 2 + 31) // 32 * 32
    T = nt * 8
    spv = nt // nv
    ring = 2 + 4 * (half - 1)
    plan, n_sem = sem_plan(nt, nz, nv)
    vmem = pl.BlockSpec(memory_space=pltpu.VMEM)
    smem = pl.BlockSpec(memory_space=pltpu.SMEM)
    hbm = pl.BlockSpec(memory_space=pl.ANY)
    V = pltpu.VMEM
    hg, head_part = pl.pallas_call(
        functools.partial(kernel, nt, nz, nv, plan, n_sem),
        out_shape=(
            jax.ShapeDtypeStruct((nt // 2, 8, width), f32),
            jax.ShapeDtypeStruct((1, rows // 2, width), bf16),
        ),
        in_specs=[vmem, vmem, hbm, smem, smem, smem],
        out_specs=(vmem, hbm),
        scratch_shapes=[
            V((nz, chip_rows, width), bf16),
            V((nz, chip_rows, T), f32),
            V((nz, R, T), f32),
            V((2 * ring, R // 4, T), f32),
            V((R, T), f32),
            V((2, nz, R, T), bf16),
            V((half, chip_rows, width), bf16),
            V((nt, 8, width), f32),
            V((nt, 8, width), f32),
            V((nt, 8, width), f32),
            V((nt // 2, 8, width), f32),
            V((8, 128), f32),
            V((8, 128), f32),
            V((nt, 8, width), f32),
            V((nt, 8, T), f32),
            V((T, width), bf16),
            V((T, width), bf16),
            V((nt, 8, T), f32),
            V((nv, 8, T), f32),
            V((nt, 8, width), f32),
            V((nt, 8, width), f32),
            V((nv, spv, 8, width), f32),
            V((nv, spv + 1, 8, width), f32),
            pltpu.SemaphoreType.DMA((nz,)),
            pltpu.SemaphoreType.DMA((half,)),
            pltpu.SemaphoreType.DMA((n_sem,)),
            pltpu.SemaphoreType.DMA((n_sem,)),
        ],
        compiler_params=pltpu.CompilerParams(
            collective_id=0, has_side_effects=True, vmem_limit_bytes=56 * 2**20),
        cost_estimate=pl.CostEstimate(
            flops=5 * rows * width * T, bytes_accessed=3 * rows * width, transcendentals=3 * R * T),
    )(hidden, norm_gain, output_head, token_ids, live_mask, advantages)
    return hg.transpose(1, 0, 2).reshape(8, nt // 2 * width), head_part


def solution(mesh):
    placed = (
        P("mp", "tok", None),
        P("mp", None),
        P("mp", "vocab", "tok"),
        P("tok"),
        P("tok"),
        P("tok"),
    )
    return jax.shard_map(
        functools.partial(per_device, mesh.shape["tok"], mesh.shape["vocab"]),
        mesh=mesh,
        in_specs=placed,
        out_specs=(P("tok", "mp"), P("mp", "vocab", "tok")),
        check_vma=False,
    )
```

time: 1310 us -> 124 us (0.09)
  blocking collectives: 1010 us -> 0 us
  waiting for transfers between devices: 230 us -> 0 us
  Pallas kernels: 0 us -> 106 us
  matrix products: 15.7 us -> 0 us
  between operations: 15.3 us -> 0.64 us
  other arithmetic: 14.5 us -> 0 us
    all_gather x3 -> x0, blocking collectives: 657 us -> none  [the longest x2 642 us: joined(): gathered = jax.tree.map(lambda a: lax.all_gather(a, axis), part)]
    psum x1 -> x0, blocking collectives: 326 us -> none  [per_device(): kl_sum = lax.psum(jnp.sum(policy_prob * lp_diff, axis=0), ('tok', 'vocab'))]
    pallas_call x0 -> x1, Pallas kernels: none -> 106 us  [per_device(): pl.pallas_call(functools.partial(kernel, nt, nz, nv, plan, n_sem), out_sh...]
    unnamed x4 -> x0, waiting for transfers between devices: 91.7 us -> none
    psum x1 -> x0, waiting for transfers between devices: 87.2 us -> none  [per_device(): summed = lax.psum(feature_grad, 'vocab')]
    all_gather x1 -> x0, waiting for transfers between devices: 35.1 us -> none  [per_device(): all_grad = lax.all_gather(logit_grad, 'tok', axis=0, tiled=True)]
    all_to_all x1 -> x0, blocking collectives: 16.7 us -> none  [per_device(): lax.all_to_all(normed, 'tok', split_axis=1, concat_axis=0, tiled=True)]
    dot_general x3 -> x0, matrix products: 15.7 us -> none  [the longest x1 6.57 us: per_device(): lax.dot_general(all_grad, weights, lead_contract, preferred_element_type=...]
  transfers between devices with their start and end apart: 7 -> 0, of which waited for: 6 -> 0; matrix products, arithmetic and copies ran while one was open for 0% -> 0% of each run, Pallas kernels for 0% -> 0%
where the time goes in v1:
time: 124 us; the launch traced here: 123 us
  Pallas kernels  106 us (85%)
  local copies, waits for them, and re-layouts  16.9 us (14%)
    pallas_call x1, Pallas kernels, per_device(): pl.pallas_call(functools.partial(kernel, nt, nz, nv, plan, n_sem), out_sh...  106 us
    unnamed x2, local copies, waits for them, and re-layouts  15.3 us

profile of v1, /device:TPU:2, one launch (start us, length us, event | category | flops | bytes accessed | tf_op | source)
XLA Modules:
  0.0 123.1 jit_solution(17523313480203333275)
XLA Ops:
  0.6 9.7 %copy.10.head = bf16[1,9600,320]{2,1,0:T(8,128)(2,1)} copy(bf16[1,9600,320]{1,2,0:T(8,128)(2,1)} %param.8) | data formatting | bytes 12288000 | tf_op args[2]
  10.3 105.5 %shard_map.77 = (f32[8,8,320]{2,1,0:T(8,128)}, bf16[1,4800,320]{2,1,0:T(8,128)(2,1)}) custom-call(bf16[1,8,5120]{2,1,0:T(8,128)(2,1)} %hidden.1, f32[1,5120]{1,0:T(1,128)} %gain.1, bf16[1,9600,320]{2,1,0:T(8,128)(2,1)} %copy.10.head, s32[8]{0:T(128)} %ids.1, s32[8]{0:T(128)} %live.1, f32[8]{0:T(128)} %adv.1), custom_call_target="tpu_custom_call" | custom-call | flops 1966080000 | bytes 9216000 | tf_op jit(solution)/shard_map/pallas_call | solution.py:545
  115.9 0.9 copy.11
  116.8 0.7 reshape.7
  117.5 5.6 %copy.12 = bf16[1,4800,320]{1,2,0:T(8,128)(2,1)} copy(bf16[1,4800,320]{2,1,0:T(8,128)(2,1)} %get-tuple-element.9) | data formatting | bytes 6144000

commit v2 on v0

v2 whole, which is shorter than its diff:
```python
import functools

import jax
import jax.numpy as jnp
from jax import lax
from jax.experimental import pallas as pl
from jax.experimental.pallas import tpu as pltpu
from jax.sharding import PartitionSpec as P

loss_scale = 256.0
kl_coef = 0.1
norm_eps = 1e-06
MESH = pl.DeviceIdType.MESH
f32 = jnp.float32
bf16 = jnp.bfloat16
LANES = 128


def pieces_of(blocks, number):
    sizes = [(blocks + number - 1 - i) // number for i in range(number)]
    starts = [sum(sizes[:i]) for i in range(number)]
    return [(a * LANES, n * LANES) for a, n in zip(starts, sizes)]


RING = 8
GATHER = 4


def sem_plan(nt, nz, nv):
    sizes = dict(
        a2a=nt, meta=nt, dw=1, unit=1, inv=1, pair=RING, up=RING * nz, down=RING * nz, peer=RING, stat=2 * nv,
        gup=GATHER * nz, gdown=GATHER * nz, gpair=GATHER * nz, fa=nt, fr=nv, fb=nv, fm=2 * nv)
    plan, count = {}, 0
    for name, size in sizes.items():
        plan[name] = count
        count += size
    return plan, count


def kernel(nt, nz, nv, plan,
           hidden, gain, head, ids, live, adv,
           hg_out, head_out,
           wbuf, lsib, lown, xbuf, rbuf, ybuf, gbuf, hbuf,
           nbuf, cbuf, ubuf, urecv, ibuf, irecv, gainb, mbuf, colb, dwb,
           stat, fbuf, fabuf, frbuf, fbb, dots,
           wsem, hsem, ss, rs):
    mp = lax.axis_index("mp")
    tok = lax.axis_index("tok")
    voc = lax.axis_index("vocab")
    zi = tok // 2
    core = tok % 2
    sib = tok + 1 - 2 * core
    half = nz // 2
    T = nt * 8
    width, vocab_dev = wbuf.shape
    kh = width // 2
    W = xbuf.shape[1]
    off = vocab_dev - W
    over = W - off
    spv = nt // nv
    rpieces = pieces_of(W // LANES, RING)
    gpieces = pieces_of(W // LANES, GATHER)
    pending = []

    def rcopy(src, dst, name, index, dev):
        at = plan[name] + index
        return pltpu.make_async_remote_copy(
            src_ref=src, dst_ref=dst, send_sem=ss.at[at], recv_sem=rs.at[at],
            device_id=dev, device_id_type=MESH)

    def begin(c):
        c.start()
        pending.append(c)

    def zat(o):
        return lax.rem(zi + o + nz, nz)

    def rows_of(o):
        return pl.ds(pl.multiple_of(zat(o) * 16, 16), 16)

    def way_dev(way):
        return {"tok": lax.rem(tok + (2 if way == "up" else nt - 2), nt)}

    def wcopy(k):
        return pltpu.make_async_copy(
            head.at[0, pl.ds(k * kh, kh), :], wbuf.at[pl.ds(k * kh, kh), :], wsem.at[k])

    for k in range(2):
        wcopy(k).start()

    barrier = pltpu.get_barrier_semaphore()

    def greet(dev):
        pl.semaphore_signal(barrier, inc=1, device_id=dev, device_id_type=MESH)

    @pl.loop(1, nt)
    def _(j):
        greet({"tok": lax.rem(tok + j, nt)})

    @pl.loop(1, nv)
    def _(j):
        greet({"vocab": lax.rem(voc + j, nv)})
        greet({"tok": sib, "vocab": lax.rem(voc + j, nv)})

    @pl.loop(0, nv)
    def _(j):
        greet({"mp": 1 - mp, "vocab": lax.rem(voc + j, nv)})

    x = hidden[0].astype(f32)
    inv = lax.rsqrt(jnp.mean(x * x, axis=1, keepdims=True) + norm_eps)
    unit = x * inv
    g = gain[...]
    normed = unit * g
    for k in range(nt):
        a = k * width
        nbuf[k] = jnp.concatenate(
            [normed[:, a:a + kh], normed[:, a + kh:a + width]], axis=0).astype(bf16)
    cbuf[tok] = nbuf[tok]

    pl.semaphore_wait(barrier, nt - 1 + 2 * (nv - 1) + nv)

    def a2a_copy(j):
        p = lax.rem(tok + j, nt)
        return rcopy(nbuf.at[p], cbuf.at[tok], "a2a", j, {"tok": p})

    def meta_copy(j):
        p = lax.rem(tok + j, nt)
        return rcopy(mbuf.at[tok], mbuf.at[tok], "meta", j, {"tok": p})

    @pl.loop(1, nt)
    def _(j):
        a2a_copy(j).start()

    for k in range(nt):
        cols = slice(k * width, (k + 1) * width)
        ubuf[k] = unit[:, cols]
        gainb[k] = jnp.broadcast_to(g[:, cols], (8, width))
    ibuf[...] = jnp.broadcast_to(inv, ibuf.shape)
    lane = lax.broadcasted_iota(jnp.int32, (8, LANES), 1)
    row = lax.broadcasted_iota(jnp.int32, (8, LANES), 0)
    info = jnp.zeros((8, LANES), f32)
    for j in range(8):
        mine = jnp.where(lane == 0, ids[j].astype(f32), jnp.where(lane == 1, live[j].astype(f32), adv[j]))
        info = jnp.where(row == j, mine, info)
    mbuf[tok] = info
    for k in range(2):
        wcopy(k).wait()

    @pl.loop(1, nt)
    def _(j):
        a2a_copy(j).wait_recv()

    cols = cbuf[...].astype(f32)
    colb[0] = cols[:, 0:8, :].reshape(T, kh).astype(bf16)
    colb[1] = cols[:, 8:16, :].reshape(T, kh).astype(bf16)

    def dot_piece(window, q):
        a, n = rpieces[q]
        at = pl.ds(pl.multiple_of(window * off + a, LANES), n)
        return jnp.dot(colb[0], wbuf[0:kh, at], preferred_element_type=f32) + jnp.dot(
            colb[1], wbuf[kh:width, at], preferred_element_type=f32)

    def lanes(q):
        a, n = rpieces[q]
        return pl.ds(a, n)

    def glanes(q):
        a, n = gpieces[q]
        return pl.ds(a, n)

    def pair_copy(q):
        return rcopy(lsib.at[:, lanes(q)], xbuf.at[:, lanes(q)], "pair", q, {"tok": sib})

    def logits(q):
        lsib[:, lanes(q)] = dot_piece(1 - core, q)
        begin(pair_copy(q))
        lown[:, lanes(q)] = dot_piece(core, q)

    def chain(way, q):
        first = half if (way == "up") == (q % 2 == 0) else half - 1
        return list(range(first, 0, -1))

    def ring_copy(way, d, q):
        o = d if way == "up" else -d
        w = 0 if way == "up" else 1
        return rcopy(
            xbuf.at[rows_of(o), lanes(q)], rbuf.at[w, d - 1, :, lanes(q)], way, (d - 1) * RING + q, way_dev(way))

    done = {}

    def peer_copy(q):
        return rcopy(xbuf.at[rows_of(0), lanes(q)], ybuf.at[:, lanes(q)], "peer", q, {"mp": 1 - mp})

    def logits_ready(q):
        pair_copy(q).wait_recv()
        xbuf[:, lanes(q)] = xbuf[:, lanes(q)] + lown[:, lanes(q)]
        for way in ("up", "down"):
            begin(ring_copy(way, chain(way, q)[0], q))
        done[q] = 0

    def step(way, q, hop):
        ds = chain(way, q)
        if hop > len(ds):
            return
        d = ds[hop - 1]
        ring_copy(way, d, q).wait_recv()
        o = d - 1 if way == "up" else 1 - d
        w = 0 if way == "up" else 1
        xbuf[rows_of(o), lanes(q)] = xbuf[rows_of(o), lanes(q)] + rbuf[w, d - 1, :, lanes(q)]
        if d > 1:
            begin(ring_copy(way, d - 1, q))
            return
        done[q] += 1
        if done[q] == 2:
            begin(peer_copy(q))

    dw_copy = rcopy(colb, dwb, "dw", 0, {"mp": 1 - mp})
    unit_copy = rcopy(ubuf.at[pl.ds(nt // 2, nt // 2)], urecv, "unit", 0, {"mp": 1 - mp})
    inv_copy = rcopy(ibuf, irecv, "inv", 0, {"mp": 1 - mp})

    def steps(hop, q):
        step("up", q, hop)
        step("down", q, hop)

    lead = 3 * RING // 4
    for q in range(RING):
        logits(q)
        if q == 0:
            for c in (dw_copy, unit_copy, inv_copy):
                begin(c)
        else:
            logits_ready(q - 1)
        if q >= lead:
            steps(1, q - lead)
    logits_ready(RING - 1)

    @pl.loop(1, nt)
    def _(j):
        meta_copy(j).start()

    for hop in range(1, half + 1):
        for q in range(RING):
            if hop > 1 or q >= RING - lead:
                steps(hop, q)

    for q in range(RING):
        peer_copy(q).wait_recv()

    own = xbuf[rows_of(0), :]
    peer = ybuf[...]
    l0 = jnp.where(mp == 0, own, peer)
    l1 = jnp.where(mp == 0, peer, own)
    lid = lax.broadcasted_iota(jnp.int32, (1, W), 1)
    counted = jnp.where((lid >= over) | (core == 0), 1.0, 0.0).astype(f32)
    lane16 = lax.broadcasted_iota(jnp.int32, (16, LANES), 1)

    def in_lanes(a, b, c):
        return jnp.where(lane16 == 0, a, jnp.where(lane16 == 1, b, c))

    h0 = jnp.max(l0, axis=1, keepdims=True)
    h1 = jnp.max(l1, axis=1, keepdims=True)
    e0 = jnp.exp(l0 - h0) * counted
    e1 = jnp.exp(l1 - h1) * counted
    me = core * nv + voc
    stat[me, 0] = in_lanes(h0, h0, h1)
    stat[me, 1] = in_lanes(
        jnp.sum(e0, axis=1, keepdims=True), jnp.sum(e0 * (l0 - l1), axis=1, keepdims=True),
        jnp.sum(e1, axis=1, keepdims=True))

    def stat_copy(other, j):
        dev = {"tok": sib if other else tok, "vocab": lax.rem(voc + j, nv)}
        return rcopy(stat.at[me], stat.at[me], "stat", other * nv + j, dev)

    @pl.loop(1, nv)
    def _(j):
        stat_copy(0, j).start()
        stat_copy(1, j).start()

    stat_copy(1, 0).start()

    @pl.loop(1, nt)
    def _(j):
        meta_copy(j).wait_recv()

    live_total = jnp.sum(jnp.sum(mbuf[...], axis=0), axis=0, keepdims=True)[:, 1:2]
    infos = mbuf[pl.ds(2 * zi, 2)].reshape(16, LANES)
    id_col = infos[:, 0:1].astype(jnp.int32)
    coef = loss_scale * infos[:, 1:2] / live_total
    adv_col = infos[:, 2:3]
    entry = voc * vocab_dev + core * off + lid
    onehot = jnp.where(entry == id_col, 1.0, 0.0).astype(f32)

    stat_copy(1, 0).wait_recv()

    @pl.loop(1, nv)
    def _(j):
        stat_copy(0, j).wait_recv()
        stat_copy(1, j).wait_recv()

    highs = stat[:, 0]
    high = jnp.max(highs, axis=0)
    total = jnp.sum(stat[:, 1] * jnp.exp(highs - high[None]), axis=0)
    log_total = jnp.log(total)
    lse0 = high[:, 0:1] + log_total[:, 0:1]
    lse1 = high[:, 2:3] + log_total[:, 2:3]
    kl = total[:, 1:2] / total[:, 0:1] - (lse0 - lse1)

    lp0 = l0 - lse0
    diff = lp0 - (l1 - lse1)
    prob = jnp.exp(lp0)
    gbuf[core, rows_of(0), :] = (
        coef * (adv_col * (prob - onehot) + kl_coef * prob * (diff - kl))).astype(bf16)

    def gchain(way, q):
        return half if (way == "up") == (q % 2 == 0) else half - 1

    def gring(way, s, q, arriving=False):
        back = s if arriving else s - 1
        view = gbuf.at[core, rows_of(-back if way == "up" else back), glanes(q)]
        return rcopy(view, view, "g" + way, (s - 1) * GATHER + q, way_dev(way))

    def gpair(o, q, arriving=False):
        view = gbuf.at[1 - core if arriving else core, rows_of(o), glanes(q)]
        return rcopy(view, view, "gpair", (o % nz) * GATHER + q, {"tok": sib})

    for q in range(GATHER):
        for way in ("up", "down"):
            if gchain(way, q) >= 1:
                begin(gring(way, 1, q))
        begin(gpair(0, q))

    def gstep(s, qs):
        for q in qs:
            for way in ("up", "down"):
                if s > gchain(way, q):
                    continue
                gring(way, s, q, True).wait_recv()
                if s < gchain(way, q):
                    begin(gring(way, s + 1, q))
                begin(gpair(-s if way == "up" else s, q))

    def gather_end(q):
        for o in range(nz):
            gpair(o, q, True).wait_recv()

    def feature(q):
        @pl.when(mp == 0)
        def _():
            a, n = gpieces[q]
            nt_dims = (((1,), (1,)), ((), ()))
            skip = over if q == 0 else 0
            part = lax.dot_general(
                gbuf[0, :, a:a + n], wbuf[:, a:a + n], nt_dims, preferred_element_type=f32)
            part = part + lax.dot_general(
                gbuf[1, :, a + skip:a + n], wbuf[:, off + a + skip:off + a + n], nt_dims,
                preferred_element_type=f32)
            part = part.reshape(nt, 8, width)
            if q == 0:
                fbuf[...] = part
            else:
                fbuf[...] = fbuf[...] + part

    every = range(GATHER)
    for s in range(1, half):
        gstep(s, every)
    gstep(half, (0,))
    for q in every:
        if q + 1 < GATHER:
            gstep(half, (q + 1,))
        gather_end(q)
        feature(q)

    def fa_copy(j):
        p = lax.rem(tok + j, nt)
        return rcopy(fbuf.at[p], fabuf.at[tok], "fa", j, {"tok": p})

    def fr_copy(j):
        p = lax.rem(voc + j, nv)
        return rcopy(fabuf.at[pl.ds(p * spv, spv)], frbuf.at[voc], "fr", j, {"vocab": p})

    target = voc // (nv // 2)

    def fb_copy(j):
        p = lax.rem(voc + j, nv)
        return rcopy(fbb.at[voc], fbb.at[voc], "fb", j, {"mp": target, "vocab": p})

    def fm_copy(j, other):
        p = lax.rem(voc + j, nv)
        return rcopy(dots.at[voc], dots.at[voc], "fm", other * nv + j, {"mp": other, "vocab": p})

    def due(j):
        return lax.rem(voc - j + nv, nv) // (nv // 2) == mp

    @pl.when(mp == 0)
    def _():
        @pl.loop(1, nt)
        def _(j):
            fa_copy(j).start()

        fabuf[tok] = fbuf[tok]

    for c in (dw_copy, unit_copy, inv_copy):
        c.wait_recv()
    n_half = vocab_dev // 2
    shift = n_half - off

    def hcopy(k):
        return pltpu.make_async_copy(
            hbuf.at[pl.ds(k * kh, kh), :], head_out.at[0, pl.ds(k * kh, kh), :], hsem.at[k])

    def head_rows(k):
        dw = jnp.where(mp == 0, colb[k].astype(f32), dwb[k].astype(f32)).T.astype(bf16)
        for a, n in gpieces:
            n = min(n, n_half - a)

            @pl.when(mp == 0)
            def _():
                hbuf[k * kh:(k + 1) * kh, a:a + n] = jnp.dot(
                    dw, gbuf[0, :, a:a + n], preferred_element_type=f32).astype(bf16)

            @pl.when(mp == 1)
            def _():
                wide = min(n + LANES, W - a)
                hbuf[k * kh:(k + 1) * kh, a:a + n] = jnp.dot(
                    dw, gbuf[1, :, a:a + wide][:, shift:shift + n], preferred_element_type=f32).astype(bf16)
        hcopy(k).start()

    head_rows(0)

    @pl.when(mp == 0)
    def _():
        @pl.loop(1, nt)
        def _(j):
            fa_copy(j).wait_recv()

        @pl.loop(1, nv)
        def _(j):
            fr_copy(j).start()

        frbuf[voc] = fabuf[pl.ds(voc * spv, spv)]

    head_rows(1)

    @pl.when(mp == 0)
    def _():
        @pl.loop(1, nv)
        def _(j):
            fr_copy(j).wait_recv()

        scaled = jnp.sum(frbuf[...], axis=0) * gainb[pl.ds(voc * spv, spv)]
        mine = ubuf[pl.ds(voc * spv, spv)] * scaled
        dot = jnp.sum(jnp.sum(mine, axis=2, keepdims=True), axis=0)
        fbb[voc] = scaled
        dots[voc] = jnp.broadcast_to(dot, (8, LANES))

        @pl.loop(1, nv)
        def _(j):
            fb_copy(j).start()
            fm_copy(j, 0).start()
            fm_copy(j, 1).start()

        fm_copy(0, 1).start()

        @pl.when(target == 1)
        def _():
            fb_copy(0).start()

        @pl.loop(1, nv)
        def _(j):
            fm_copy(j, 0).wait_recv()

            @pl.when(due(j))
            def _():
                fb_copy(j).wait_recv()

    @pl.when(mp == 1)
    def _():
        @pl.loop(0, nv)
        def _(j):
            fm_copy(j, 1).wait_recv()

            @pl.when(due(j))
            def _():
                fb_copy(j).wait_recv()

    mean = jnp.sum(dots[...], axis=0)[:, 0:1] * (1.0 / (nt * width))
    inv_pol = jnp.where(mp == 0, ibuf[:, 0:1], irecv[:, 0:1])
    for i in range(nt // 2):
        slab = mp * (nt // 2) + i
        unit_pol = jnp.where(mp == 0, ubuf[i], urecv[i])
        hg_out[:, i * width:(i + 1) * width] = inv_pol * (
            fbb[slab // spv, lax.rem(slab, spv)] - unit_pol * mean)

    for k in range(2):
        hcopy(k).wait()
    for c in pending:
        c.wait_send()

    @pl.loop(1, nt)
    def _(j):
        a2a_copy(j).wait_send()
        meta_copy(j).wait_send()

    stat_copy(1, 0).wait_send()

    @pl.loop(1, nv)
    def _(j):
        stat_copy(0, j).wait_send()
        stat_copy(1, j).wait_send()

    @pl.when(mp == 0)
    def _():
        @pl.loop(1, nt)
        def _(j):
            fa_copy(j).wait_send()

        @pl.loop(1, nv)
        def _(j):
            fr_copy(j).wait_send()
            fb_copy(j).wait_send()
            fm_copy(j, 0).wait_send()
            fm_copy(j, 1).wait_send()

        fm_copy(0, 1).wait_send()

        @pl.when(target == 1)
        def _():
            fb_copy(0).wait_send()


def per_device(nt, nv, hidden, norm_gain, output_head, token_ids, live_mask, advantages):
    nz = nt // 2
    half = nz // 2
    rows, width = output_head.shape[1:]
    kh = width // 2
    blocks = rows // LANES
    W = (blocks + 1) // 2 * LANES
    T = nt * 8
    spv = nt // nv
    plan, n_sem = sem_plan(nt, nz, nv)
    vmem = pl.BlockSpec(memory_space=pltpu.VMEM)
    smem = pl.BlockSpec(memory_space=pltpu.SMEM)
    hbm = pl.BlockSpec(memory_space=pl.ANY)
    V = pltpu.VMEM
    hg, head_part = pl.pallas_call(
        functools.partial(kernel, nt, nz, nv, plan),
        out_shape=(
            jax.ShapeDtypeStruct((8, nt // 2 * width), f32),
            jax.ShapeDtypeStruct((1, width, rows // 2), bf16),
        ),
        in_specs=[vmem, vmem, hbm, smem, smem, smem],
        out_specs=(vmem, hbm),
        scratch_shapes=[
            V((width, rows), bf16),
            V((T, W), f32),
            V((T, W), f32),
            V((T, W), f32),
            V((2, half, 16, W), f32),
            V((16, W), f32),
            V((2, T, W), bf16),
            V((width, rows // 2), bf16),
            V((nt, 16, kh), bf16),
            V((nt, 16, kh), bf16),
            V((nt, 8, width), f32),
            V((nt // 2, 8, width), f32),
            V((8, LANES), f32),
            V((8, LANES), f32),
            V((nt, 8, width), f32),
            V((nt, 8, LANES), f32),
            V((2, T, kh), bf16),
            V((2, T, kh), bf16),
            V((2 * nv, 2, 16, LANES), f32),
            V((nt, 8, width), f32),
            V((nt, 8, width), f32),
            V((nv, spv, 8, width), f32),
            V((nv, spv, 8, width), f32),
            V((nv, 8, LANES), f32),
            pltpu.SemaphoreType.DMA((2,)),
            pltpu.SemaphoreType.DMA((2,)),
            pltpu.SemaphoreType.DMA((n_sem,)),
            pltpu.SemaphoreType.DMA((n_sem,)),
        ],
        compiler_params=pltpu.CompilerParams(
            collective_id=0, has_side_effects=True, vmem_limit_bytes=56 * 2**20),
        cost_estimate=pl.CostEstimate(
            flops=5 * rows * width * T, bytes_accessed=3 * rows * width, transcendentals=3 * 16 * W),
    )(hidden, norm_gain, jnp.swapaxes(output_head, 1, 2), token_ids, live_mask, advantages)
    return hg, jnp.swapaxes(head_part, 1, 2)


def solution(mesh):
    placed = (
        P("mp", "tok", None),
        P("mp", None),
        P("mp", "vocab", "tok"),
        P("tok"),
        P("tok"),
        P("tok"),
    )
    return jax.shard_map(
        functools.partial(per_device, mesh.shape["tok"], mesh.shape["vocab"]),
        mesh=mesh,
        in_specs=placed,
        out_specs=(P("tok", "mp"), P("mp", "vocab", "tok")),
        check_vma=False,
    )
```

time: 1310 us -> 107 us (0.08)
  blocking collectives: 1010 us -> 0 us
  waiting for transfers between devices: 230 us -> 0 us
  Pallas kernels: 0 us -> 101 us
  matrix products: 15.7 us -> 0 us
  between operations: 15.3 us -> 0.64 us
  other arithmetic: 14.5 us -> 0 us
    all_gather x3 -> x0, blocking collectives: 657 us -> none  [the longest x2 642 us: joined(): gathered = jax.tree.map(lambda a: lax.all_gather(a, axis), part)]
    psum x1 -> x0, blocking collectives: 326 us -> none  [per_device(): kl_sum = lax.psum(jnp.sum(policy_prob * lp_diff, axis=0), ('tok', 'vocab'))]
    pallas_call x0 -> x1, Pallas kernels: none -> 101 us  [per_device(): pl.pallas_call(functools.partial(kernel, nt, nz, nv, plan), out_shape=(ja...]
    unnamed x4 -> x0, waiting for transfers between devices: 91.7 us -> none
    psum x1 -> x0, waiting for transfers between devices: 87.2 us -> none  [per_device(): summed = lax.psum(feature_grad, 'vocab')]
    all_gather x1 -> x0, waiting for transfers between devices: 35.1 us -> none  [per_device(): all_grad = lax.all_gather(logit_grad, 'tok', axis=0, tiled=True)]
    all_to_all x1 -> x0, blocking collectives: 16.7 us -> none  [per_device(): lax.all_to_all(normed, 'tok', split_axis=1, concat_axis=0, tiled=True)]
    dot_general x3 -> x0, matrix products: 15.7 us -> none  [the longest x1 6.57 us: per_device(): lax.dot_general(all_grad, weights, lead_contract, preferred_element_type=...]
  transfers between devices with their start and end apart: 7 -> 0, of which waited for: 6 -> 0; matrix products, arithmetic and copies ran while one was open for 0% -> 0% of each run, Pallas kernels for 0% -> 0%
where the time goes in v2:
time: 107 us
  Pallas kernels  101 us (94%)
  local copies, waits for them, and re-layouts  5.26 us (5%)
    pallas_call x1, Pallas kernels, per_device(): pl.pallas_call(functools.partial(kernel, nt, nz, nv, plan), out_shape=(ja...  101 us
    unnamed x2, local copies, waits for them, and re-layouts  5.26 us

profile of v2, /device:TPU:2, one launch (start us, length us, event | category | flops | bytes accessed | tf_op | source)
XLA Modules:
  0.0 107.0 jit_solution(16386334550131728729)
XLA Ops:
  0.6 101.1 %shard_map.77 = (f32[8,2560]{1,0:T(8,128)}, bf16[1,320,4800]{2,1,0:T(8,128)(2,1)}) custom-call(bf16[1,8,5120]{2,1,0:T(8,128)(2,1)} %hidden.1, f32[1,5120]{1,0:T(1,128)} %gain.1, bf16[1,320,9600]{2,1,0:T(8,128)(2,1)} %bitcast.3, s32[8]{0:T(128)} %ids.1, s32[8]{0:T(128)} %live.1, f32[8]{0:T(128)} %adv.1), custom_call_target="tpu_custom_call" | custom-call | flops 1966080000 | bytes 9216000 | tf_op jit(solution)/shard_map/pallas_call | solution.py:545
  101.7 1.5 %copy.10 = f32[8,2560]{1,0:T(8,128)} copy(f32[8,2560]{1,0:T(8,128)} %get-tuple-element.8) | data formatting | bytes 163840
  103.2 3.7 %copy.11 = bf16[1,4800,320]{1,2,0:T(8,128)(2,1)} copy(bf16[1,4800,320]{1,2,0:T(8,128)(2,1)} %bitcast.2) | data formatting | bytes 6144000

commit v3 on v2

--- a/solution.py
+++ b/solution.py
@@ -23,13 +23,14 @@
 
 
 RING = 8
-GATHER = 4
+TURNS = 2
+HEAD_PARTS = 4
 
 
 def sem_plan(nt, nz, nv):
     sizes = dict(
-        a2a=nt, meta=nt, dw=1, unit=1, inv=1, pair=RING, up=RING * nz, down=RING * nz, peer=RING, stat=2 * nv,
-        gup=GATHER * nz, gdown=GATHER * nz, gpair=GATHER * nz, fa=nt, fr=nv, fb=nv, fm=2 * nv)
+        a2a=nt, meta=nt, dw=1, unit=1, inv=1, pair=RING, up=RING * nz, down=RING * nz, peer=RING, stat=2 * nv, gs=2 * TURNS * nz,
+        gz=TURNS * nz, gx=TURNS * nz, gxs=TURNS * nz, fa=nt, fr=nv, fb=nv, fm=2 * nv)
     plan, count = {}, 0
     for name, size in sizes.items():
         plan[name] = count
@@ -54,12 +55,15 @@
     T = nt * 8
     width, vocab_dev = wbuf.shape
     kh = width // 2
-    W = xbuf.shape[1]
+    W = gbuf.shape[2]
     off = vocab_dev - W
     over = W - off
     spv = nt // nv
     rpieces = pieces_of(W // LANES, RING)
-    gpieces = pieces_of(W // LANES, GATHER)
+    turns = pieces_of(W // LANES // 2, TURNS)
+    hpieces = pieces_of(W // LANES, HEAD_PARTS)
+    active = mp == core
+    held = {}
     pending = []
 
     def rcopy(src, dst, name, index, dev):
@@ -72,6 +76,10 @@
         c.start()
         pending.append(c)
 
+    def begin_if(when, make, *at):
+        make(*at).start()
+        held.setdefault(when, []).append((make, at))
+
     def zat(o):
         return lax.rem(zi + o + nz, nz)
 
@@ -100,11 +108,11 @@
     @pl.loop(1, nv)
     def _(j):
         greet({"vocab": lax.rem(voc + j, nv)})
-        greet({"tok": sib, "vocab": lax.rem(voc + j, nv)})
 
     @pl.loop(0, nv)
     def _(j):
         greet({"mp": 1 - mp, "vocab": lax.rem(voc + j, nv)})
+        greet({"mp": 1 - mp, "tok": sib, "vocab": lax.rem(voc + j, nv)})
 
     x = hidden[0].astype(f32)
     inv = lax.rsqrt(jnp.mean(x * x, axis=1, keepdims=True) + norm_eps)
@@ -117,7 +125,7 @@
             [normed[:, a:a + kh], normed[:, a + kh:a + width]], axis=0).astype(bf16)
     cbuf[tok] = nbuf[tok]
 
-    pl.semaphore_wait(barrier, nt - 1 + 2 * (nv - 1) + nv)
+    pl.semaphore_wait(barrier, nt - 1 + nv - 1 + 2 * nv)
 
     def a2a_copy(j):
         p = lax.rem(tok + j, nt)
@@ -161,20 +169,19 @@
             colb[1], wbuf[kh:width, at], preferred_element_type=f32)
 
     def lanes(q):
-        a, n = rpieces[q]
-        return pl.ds(a, n)
-
-    def glanes(q):
-        a, n = gpieces[q]
-        return pl.ds(a, n)
+        return pl.ds(0, rpieces[q][1])
+
+    def glanes(i, who):
+        a, n = turns[i]
+        return pl.ds(pl.multiple_of(2 * a + who * n, LANES), n)
 
     def pair_copy(q):
-        return rcopy(lsib.at[:, lanes(q)], xbuf.at[:, lanes(q)], "pair", q, {"tok": sib})
+        return rcopy(lsib.at[q, :, lanes(q)], xbuf.at[q, :, lanes(q)], "pair", q, {"tok": sib})
 
     def logits(q):
-        lsib[:, lanes(q)] = dot_piece(1 - core, q)
+        lsib[q, :, lanes(q)] = dot_piece(1 - core, q)
         begin(pair_copy(q))
-        lown[:, lanes(q)] = dot_piece(core, q)
+        lown[q, :, lanes(q)] = dot_piece(core, q)
 
     def chain(way, q):
         first = half if (way == "up") == (q % 2 == 0) else half - 1
@@ -184,16 +191,16 @@
         o = d if way == "up" else -d
         w = 0 if way == "up" else 1
         return rcopy(
-            xbuf.at[rows_of(o), lanes(q)], rbuf.at[w, d - 1, :, lanes(q)], way, (d - 1) * RING + q, way_dev(way))
+            xbuf.at[q, rows_of(o), lanes(q)], rbuf.at[w, d - 1, q, :, lanes(q)], way, (d - 1) * RING + q, way_dev(way))
 
     done = {}
 
     def peer_copy(q):
-        return rcopy(xbuf.at[rows_of(0), lanes(q)], ybuf.at[:, lanes(q)], "peer", q, {"mp": 1 - mp})
+        return rcopy(xbuf.at[q, rows_of(0), lanes(q)], ybuf.at[q, :, lanes(q)], "peer", q, {"mp": 1 - mp})
 
     def logits_ready(q):
         pair_copy(q).wait_recv()
-        xbuf[:, lanes(q)] = xbuf[:, lanes(q)] + lown[:, lanes(q)]
+        xbuf[q, :, lanes(q)] = xbuf[q, :, lanes(q)] + lown[q, :, lanes(q)]
         for way in ("up", "down"):
             begin(ring_copy(way, chain(way, q)[0], q))
         done[q] = 0
@@ -206,13 +213,15 @@
         ring_copy(way, d, q).wait_recv()
         o = d - 1 if way == "up" else 1 - d
         w = 0 if way == "up" else 1
-        xbuf[rows_of(o), lanes(q)] = xbuf[rows_of(o), lanes(q)] + rbuf[w, d - 1, :, lanes(q)]
+        xbuf[q, rows_of(o), lanes(q)] = xbuf[q, rows_of(o), lanes(q)] + rbuf[w, d - 1, q, :, lanes(q)]
         if d > 1:
             begin(ring_copy(way, d - 1, q))
             return
         done[q] += 1
         if done[q] == 2:
-            begin(peer_copy(q))
+            @pl.when(jnp.logical_not(active))
+            def _():
+                begin_if("idle", peer_copy, q)
 
     dw_copy = rcopy(colb, dwb, "dw", 0, {"mp": 1 - mp})
     unit_copy = rcopy(ubuf.at[pl.ds(nt // 2, nt // 2)], urecv, "unit", 0, {"mp": 1 - mp})
@@ -243,132 +252,179 @@
             if hop > 1 or q >= RING - lead:
                 steps(hop, q)
 
-    for q in range(RING):
-        peer_copy(q).wait_recv()
-
-    own = xbuf[rows_of(0), :]
-    peer = ybuf[...]
-    l0 = jnp.where(mp == 0, own, peer)
-    l1 = jnp.where(mp == 0, peer, own)
-    lid = lax.broadcasted_iota(jnp.int32, (1, W), 1)
-    counted = jnp.where((lid >= over) | (core == 0), 1.0, 0.0).astype(f32)
-    lane16 = lax.broadcasted_iota(jnp.int32, (16, LANES), 1)
-
-    def in_lanes(a, b, c):
-        return jnp.where(lane16 == 0, a, jnp.where(lane16 == 1, b, c))
-
-    h0 = jnp.max(l0, axis=1, keepdims=True)
-    h1 = jnp.max(l1, axis=1, keepdims=True)
-    e0 = jnp.exp(l0 - h0) * counted
-    e1 = jnp.exp(l1 - h1) * counted
-    me = core * nv + voc
-    stat[me, 0] = in_lanes(h0, h0, h1)
-    stat[me, 1] = in_lanes(
-        jnp.sum(e0, axis=1, keepdims=True), jnp.sum(e0 * (l0 - l1), axis=1, keepdims=True),
-        jnp.sum(e1, axis=1, keepdims=True))
+    @pl.loop(1, nt)
+    def _(j):
+        meta_copy(j).wait_recv()
+
+    me = mp * nv + voc
 
     def stat_copy(other, j):
-        dev = {"tok": sib if other else tok, "vocab": lax.rem(voc + j, nv)}
+        dev = {"vocab": lax.rem(voc + j, nv)}
+        if other:
+            dev.update({"mp": 1 - mp, "tok": sib})
         return rcopy(stat.at[me], stat.at[me], "stat", other * nv + j, dev)
 
-    @pl.loop(1, nv)
-    def _(j):
-        stat_copy(0, j).start()
-        stat_copy(1, j).start()
-
-    stat_copy(1, 0).start()
-
-    @pl.loop(1, nt)
-    def _(j):
-        meta_copy(j).wait_recv()
-
-    live_total = jnp.sum(jnp.sum(mbuf[...], axis=0), axis=0, keepdims=True)[:, 1:2]
-    infos = mbuf[pl.ds(2 * zi, 2)].reshape(16, LANES)
-    id_col = infos[:, 0:1].astype(jnp.int32)
-    coef = loss_scale * infos[:, 1:2] / live_total
-    adv_col = infos[:, 2:3]
-    entry = voc * vocab_dev + core * off + lid
-    onehot = jnp.where(entry == id_col, 1.0, 0.0).astype(f32)
-
-    stat_copy(1, 0).wait_recv()
-
-    @pl.loop(1, nv)
-    def _(j):
-        stat_copy(0, j).wait_recv()
-        stat_copy(1, j).wait_recv()
-
-    highs = stat[:, 0]
-    high = jnp.max(highs, axis=0)
-    total = jnp.sum(stat[:, 1] * jnp.exp(highs - high[None]), axis=0)
-    log_total = jnp.log(total)
-    lse0 = high[:, 0:1] + log_total[:, 0:1]
-    lse1 = high[:, 2:3] + log_total[:, 2:3]
-    kl = total[:, 1:2] / total[:, 0:1] - (lse0 - lse1)
-
-    lp0 = l0 - lse0
-    diff = lp0 - (l1 - lse1)
-    prob = jnp.exp(lp0)
-    gbuf[core, rows_of(0), :] = (
-        coef * (adv_col * (prob - onehot) + kl_coef * prob * (diff - kl))).astype(bf16)
-
-    def gchain(way, q):
-        return half if (way == "up") == (q % 2 == 0) else half - 1
-
-    def gring(way, s, q, arriving=False):
-        back = s if arriving else s - 1
-        view = gbuf.at[core, rows_of(-back if way == "up" else back), glanes(q)]
-        return rcopy(view, view, "g" + way, (s - 1) * GATHER + q, way_dev(way))
-
-    def gpair(o, q, arriving=False):
-        view = gbuf.at[1 - core if arriving else core, rows_of(o), glanes(q)]
-        return rcopy(view, view, "gpair", (o % nz) * GATHER + q, {"tok": sib})
-
-    for q in range(GATHER):
-        for way in ("up", "down"):
-            if gchain(way, q) >= 1:
-                begin(gring(way, 1, q))
-        begin(gpair(0, q))
-
-    def gstep(s, qs):
-        for q in qs:
-            for way in ("up", "down"):
-                if s > gchain(way, q):
-                    continue
-                gring(way, s, q, True).wait_recv()
-                if s < gchain(way, q):
-                    begin(gring(way, s + 1, q))
-                begin(gpair(-s if way == "up" else s, q))
-
-    def gather_end(q):
-        for o in range(nz):
-            gpair(o, q, True).wait_recv()
-
-    def feature(q):
+    def gs_copy(o, i, who):
+        view = gbuf.at[mp, rows_of(o), glanes(i, who)]
+        return rcopy(view, view, "gs", ((o % nz) * TURNS + i) * 2 + (0 if o else who), {"tok": sib})
+
+    @pl.when(active)
+    def _():
+        for q in range(RING):
+            peer_copy(q).wait_recv()
+
+        own = jnp.concatenate([xbuf[q, rows_of(0), lanes(q)] for q in range(RING)], axis=1)
+        peer = jnp.concatenate([ybuf[q, :, lanes(q)] for q in range(RING)], axis=1)
+        l0 = jnp.where(mp == 0, own, peer)
+        l1 = jnp.where(mp == 0, peer, own)
+        lid = lax.broadcasted_iota(jnp.int32, (1, W), 1)
+        counted = jnp.where((lid >= over) | (core == 0), 1.0, 0.0).astype(f32)
+        lane16 = lax.broadcasted_iota(jnp.int32, (16, LANES), 1)
+
+        def in_lanes(a, b, c):
+            return jnp.where(lane16 == 0, a, jnp.where(lane16 == 1, b, c))
+
+        h0 = jnp.max(l0, axis=1, keepdims=True)
+        h1 = jnp.max(l1, axis=1, keepdims=True)
+        e0 = jnp.exp(l0 - h0) * counted
+        e1 = jnp.exp(l1 - h1) * counted
+        stat[me, 0] = in_lanes(h0, h0, h1)
+        stat[me, 1] = in_lanes(
+            jnp.sum(e0, axis=1, keepdims=True), jnp.sum(e0 * (l0 - l1), axis=1, keepdims=True),
+            jnp.sum(e1, axis=1, keepdims=True))
+
+        @pl.loop(1, nv)
+        def _(j):
+            stat_copy(0, j).start()
+            stat_copy(1, j).start()
+
+        stat_copy(1, 0).start()
+
+        live_total = jnp.sum(jnp.sum(mbuf[...], axis=0), axis=0, keepdims=True)[:, 1:2]
+        infos = mbuf[pl.ds(2 * zi, 2)].reshape(16, LANES)
+        id_col = infos[:, 0:1].astype(jnp.int32)
+        coef = loss_scale * infos[:, 1:2] / live_total
+        adv_col = infos[:, 2:3]
+        entry = voc * vocab_dev + core * off + lid
+        onehot = jnp.where(entry == id_col, 1.0, 0.0).astype(f32)
+
+        stat_copy(1, 0).wait_recv()
+
+        @pl.loop(1, nv)
+        def _(j):
+            stat_copy(0, j).wait_recv()
+            stat_copy(1, j).wait_recv()
+
+        highs = stat[:, 0]
+        high = jnp.max(highs, axis=0)
+        total = jnp.sum(stat[:, 1] * jnp.exp(highs - high[None]), axis=0)
+        log_total = jnp.log(total)
+        lse0 = high[:, 0:1] + log_total[:, 0:1]
+        lse1 = high[:, 2:3] + log_total[:, 2:3]
+        kl = total[:, 1:2] / total[:, 0:1] - (lse0 - lse1)
+
+        lp0 = l0 - lse0
+        diff = lp0 - (l1 - lse1)
+        prob = jnp.exp(lp0)
+        gbuf[mp, rows_of(0), :] = (
+            coef * (adv_col * (prob - onehot) + kl_coef * prob * (diff - kl))).astype(bf16)
+        for i in range(TURNS):
+            for who in (0, 1):
+                begin_if("active", gs_copy, 0, i, who)
+
+    @pl.when(jnp.logical_not(active))
+    def _():
+        for i in range(TURNS):
+            for who in (0, 1):
+                gs_copy(0, i, who).wait_recv()
+
+    def gz_copy(o, i, to):
+        view = gbuf.at[mp, rows_of(o), glanes(i, core)]
+        return rcopy(view, view, "gz", ((o - to) % nz) * TURNS + i, {"tok": lax.rem(tok + 2 * to + nt, nt)})
+
+    def gz_arrival(o, i):
+        view = gbuf.at[mp, rows_of(o), glanes(i, core)]
+        return rcopy(view, view, "gz", (o % nz) * TURNS + i, {"tok": tok})
+
+    def gx_copy(o, i):
+        view = gbuf.at[1, rows_of(o), glanes(i, core)]
+        return rcopy(view, view, "gx", (o % nz) * TURNS + i, {"mp": 1 - mp})
+
+    def gxs_copy(o, i, who):
+        view = gbuf.at[1, rows_of(o), glanes(i, who)]
+        return rcopy(view, view, "gxs", (o % nz) * TURNS + i, {"tok": sib})
+
+    def sides(d, i):
+        if d == half:
+            return (-1,) if i % 2 == 0 else (1,)
+        return (-1, 1)
+
+    def over_x(o, i):
+        @pl.when(mp == 1)
+        def _():
+            begin_if("ref", gx_copy, o, i)
+
+    for d in range(1, min(2, half) + 1):
+        for i in range(TURNS):
+            for side in sides(d, i):
+                begin(gz_copy(0, i, -side * d))
+    for i in range(TURNS):
+        over_x(0, i)
+
+    def along(d):
+        for i in range(TURNS):
+            for side in sides(d, i):
+                o = side * d
+                gz_arrival(o, i).wait_recv()
+                if d == 2:
+                    for more in range(3, half + 1):
+                        if side in sides(more, i):
+                            begin(gz_copy(o, i, -side * (more - 2)))
+                begin(gs_copy(o, i, core))
+                over_x(o, i)
+
+    def across(d):
         @pl.when(mp == 0)
         def _():
-            a, n = gpieces[q]
-            nt_dims = (((1,), (1,)), ((), ()))
-            skip = over if q == 0 else 0
+            for i in range(TURNS):
+                for side in sides(d, i) if d else (1,):
+                    gx_copy(side * d, i).wait_recv()
+                    begin_if("policy", gxs_copy, side * d, i, core)
+
+    def sib_end(i):
+        for o in range(1, nz):
+            gs_copy(o, i, 1 - core).wait_recv()
+
+    def feature(window, i):
+        @pl.when(mp == 0)
+        def _():
+            if window == 1:
+                for o in range(nz):
+                    gxs_copy(o, i, 1 - core).wait_recv()
+            a, n = turns[i]
+            a, n = 2 * a, 2 * n
+            skip = over if window == 1 and i == 0 else 0
+            first = window * off
             part = lax.dot_general(
-                gbuf[0, :, a:a + n], wbuf[:, a:a + n], nt_dims, preferred_element_type=f32)
-            part = part + lax.dot_general(
-                gbuf[1, :, a + skip:a + n], wbuf[:, off + a + skip:off + a + n], nt_dims,
-                preferred_element_type=f32)
-            part = part.reshape(nt, 8, width)
-            if q == 0:
+                gbuf[window, :, a + skip:a + n], wbuf[:, first + a + skip:first + a + n],
+                (((1,), (1,)), ((), ())), preferred_element_type=f32).reshape(nt, 8, width)
+            if window == 0 and i == 0:
                 fbuf[...] = part
             else:
                 fbuf[...] = fbuf[...] + part
 
-    every = range(GATHER)
-    for s in range(1, half):
-        gstep(s, every)
-    gstep(half, (0,))
-    for q in every:
-        if q + 1 < GATHER:
-            gstep(half, (q + 1,))
-        gather_end(q)
-        feature(q)
+    for d in range(1, half + 1):
+        along(d)
+        if d >= 2:
+            across(d - 2)
+    across(half - 1)
+    for i in range(TURNS):
+        sib_end(i)
+        feature(0, i)
+        if i == 0:
+            across(half)
+    for i in range(TURNS):
+        feature(1, i)
 
     def fa_copy(j):
         p = lax.rem(tok + j, nt)
@@ -410,7 +466,7 @@
 
     def head_rows(k):
         dw = jnp.where(mp == 0, colb[k].astype(f32), dwb[k].astype(f32)).T.astype(bf16)
-        for a, n in gpieces:
+        for a, n in hpieces:
             n = min(n, n_half - a)
 
             @pl.when(mp == 0)
@@ -501,12 +557,21 @@
         a2a_copy(j).wait_send()
         meta_copy(j).wait_send()
 
-    stat_copy(1, 0).wait_send()
-
-    @pl.loop(1, nv)
-    def _(j):
-        stat_copy(0, j).wait_send()
-        stat_copy(1, j).wait_send()
+    @pl.when(active)
+    def _():
+        stat_copy(1, 0).wait_send()
+
+        @pl.loop(1, nv)
+        def _(j):
+            stat_copy(0, j).wait_send()
+            stat_copy(1, j).wait_send()
+
+    for name, cond in (
+            ("active", active), ("idle", jnp.logical_not(active)), ("ref", mp == 1), ("policy", mp == 0)):
+        @pl.when(cond)
+        def _():
+            for make, at in held[name]:
+                make(*at).wait_send()
 
     @pl.when(mp == 0)
     def _():
@@ -535,6 +600,7 @@
     kh = width // 2
     blocks = rows // LANES
     W = (blocks + 1) // 2 * LANES
+    piece = pieces_of(W // LANES, RING)[0][1]
     T = nt * 8
     spv = nt // nv
     plan, n_sem = sem_plan(nt, nz, nv)
@@ -552,11 +618,11 @@
         out_specs=(vmem, hbm),
         scratch_shapes=[
             V((width, rows), bf16),
-            V((T, W), f32),
-            V((T, W), f32),
-            V((T, W), f32),
-            V((2, half, 16, W), f32),
-            V((16, W), f32),
+            V((RING, T, piece), f32),
+            V((RING, T, piece), f32),
+            V((RING, T, piece), f32),
+            V((2, half, RING, 16, piece), f32),
+            V((RING, 16, piece), f32),
             V((2, T, W), bf16),
             V((width, rows // 2), bf16),
             V((nt, 16, kh), bf16),

time: 107 us -> 106 us (level)
  Pallas kernels: 101 us -> 99.7 us
    pallas_call x1, Pallas kernels: 101 us -> 99.7 us  [per_device(): pl.pallas_call(functools.partial(kernel, nt, nz, nv, plan), out_shape=(ja...]
where the time goes in v3:
time: 106 us
  Pallas kernels  99.7 us (94%)
  local copies, waits for them, and re-layouts  5.26 us (5%)
    pallas_call x1, Pallas kernels, per_device(): pl.pallas_call(functools.partial(kernel, nt, nz, nv, plan), out_shape=(ja...  99.7 us
    unnamed x2, local copies, waits for them, and re-layouts  5.26 us

profile of v3, /device:TPU:2, one launch (start us, length us, event | category | flops | bytes accessed | tf_op | source)
XLA Modules:
  0.0 105.6 jit_solution(7203877836513192659)
XLA Ops:
  0.6 99.7 %shard_map.77 = (f32[8,2560]{1,0:T(8,128)}, bf16[1,320,4800]{2,1,0:T(8,128)(2,1)}) custom-call(bf16[1,8,5120]{2,1,0:T(8,128)(2,1)} %hidden.1, f32[1,5120]{1,0:T(1,128)} %gain.1, bf16[1,320,9600]{2,1,0:T(8,128)(2,1)} %bitcast.3, s32[8]{0:T(128)} %ids.1, s32[8]{0:T(128)} %live.1, f32[8]{0:T(128)} %adv.1), custom_call_target="tpu_custom_call" | custom-call | flops 1966080000 | bytes 9216000 | tf_op jit(solution)/shard_map/pallas_call | solution.py:611
  100.3 1.5 %copy.10 = f32[8,2560]{1,0:T(8,128)} copy(f32[8,2560]{1,0:T(8,128)} %get-tuple-element.8) | data formatting | bytes 163840
  101.9 3.7 %copy.11 = bf16[1,4800,320]{1,2,0:T(8,128)(2,1)} copy(bf16[1,4800,320]{1,2,0:T(8,128)(2,1)} %bitcast.2) | data formatting | bytes 6144000

commit v4 on v3

--- a/solution.py
+++ b/solution.py
@@ -24,6 +24,8 @@
 
 RING = 8
 TURNS = 2
+LEAD = 5
+READY = 2
 HEAD_PARTS = 4
 
 
@@ -151,6 +153,11 @@
         mine = jnp.where(lane == 0, ids[j].astype(f32), jnp.where(lane == 1, live[j].astype(f32), adv[j]))
         info = jnp.where(row == j, mine, info)
     mbuf[tok] = info
+
+    @pl.loop(1, nt)
+    def _(j):
+        meta_copy(j).start()
+
     for k in range(2):
         wcopy(k).wait()
 
@@ -231,21 +238,18 @@
         step("up", q, hop)
         step("down", q, hop)
 
-    lead = 3 * RING // 4
+    lead = LEAD
     for q in range(RING):
         logits(q)
-        if q == 0:
+        if q >= READY:
+            logits_ready(q - READY)
+        if q == 3:
             for c in (dw_copy, unit_copy, inv_copy):
                 begin(c)
-        else:
-            logits_ready(q - 1)
         if q >= lead:
             steps(1, q - lead)
-    logits_ready(RING - 1)
-
-    @pl.loop(1, nt)
-    def _(j):
-        meta_copy(j).start()
+    for q in range(RING - READY, RING):
+        logits_ready(q)
 
     for hop in range(1, half + 1):
         for q in range(RING):

time: 106 us -> 104 us (0.981)
  Pallas kernels: 99.7 us -> 98.3 us
    pallas_call x1, Pallas kernels: 99.7 us -> 98.3 us  [per_device(): pl.pallas_call(functools.partial(kernel, nt, nz, nv, plan), out_shape=(ja...]
where the time goes in v4:
time: 104 us
  Pallas kernels  98.3 us (95%)
  local copies, waits for them, and re-layouts  5.26 us (5%)
    pallas_call x1, Pallas kernels, per_device(): pl.pallas_call(functools.partial(kernel, nt, nz, nv, plan), out_shape=(ja...  98.3 us
    unnamed x2, local copies, waits for them, and re-layouts  5.26 us

profile of v4, /device:TPU:2, one launch (start us, length us, event | category | flops | bytes accessed | tf_op | source)
XLA Modules:
  0.0 104.2 jit_solution(17275888892424809576)
XLA Ops:
  0.6 98.3 %shard_map.77 = (f32[8,2560]{1,0:T(8,128)}, bf16[1,320,4800]{2,1,0:T(8,128)(2,1)}) custom-call(bf16[1,8,5120]{2,1,0:T(8,128)(2,1)} %hidden.1, f32[1,5120]{1,0:T(1,128)} %gain.1, bf16[1,320,9600]{2,1,0:T(8,128)(2,1)} %bitcast.3, s32[8]{0:T(128)} %ids.1, s32[8]{0:T(128)} %live.1, f32[8]{0:T(128)} %adv.1), custom_call_target="tpu_custom_call" | custom-call | flops 1966080000 | bytes 9216000 | tf_op jit(solution)/shard_map/pallas_call | solution.py:615
  98.9 1.5 %copy.10 = f32[8,2560]{1,0:T(8,128)} copy(f32[8,2560]{1,0:T(8,128)} %get-tuple-element.8) | data formatting | bytes 163840
  100.5 3.7 %copy.11 = bf16[1,4800,320]{1,2,0:T(8,128)(2,1)} copy(bf16[1,4800,320]{1,2,0:T(8,128)(2,1)} %bitcast.2) | data formatting | bytes 6144000

commit v5 on v4

--- a/solution.py
+++ b/solution.py
@@ -23,7 +23,7 @@
 
 
 RING = 8
-TURNS = 2
+TURNS = 1
 LEAD = 5
 READY = 2
 HEAD_PARTS = 4

time: 104 us -> 105 us (level)
  no operation moved by 1% of the time
where the time goes in v5:
time: 105 us
  Pallas kernels  99.1 us (94%)
  local copies, waits for them, and re-layouts  5.26 us (5%)
    pallas_call x1, Pallas kernels, per_device(): pl.pallas_call(functools.partial(kernel, nt, nz, nv, plan), out_shape=(ja...  99.1 us
    unnamed x2, local copies, waits for them, and re-layouts  5.26 us

profile of v5, /device:TPU:2, one launch (start us, length us, event | category | flops | bytes accessed | tf_op | source)
XLA Modules:
  0.0 105.0 jit_solution(7028273072161805299)
XLA Ops:
  0.6 99.1 %shard_map.77 = (f32[8,2560]{1,0:T(8,128)}, bf16[1,320,4800]{2,1,0:T(8,128)(2,1)}) custom-call(bf16[1,8,5120]{2,1,0:T(8,128)(2,1)} %hidden.1, f32[1,5120]{1,0:T(1,128)} %gain.1, bf16[1,320,9600]{2,1,0:T(8,128)(2,1)} %bitcast.3, s32[8]{0:T(128)} %ids.1, s32[8]{0:T(128)} %live.1, f32[8]{0:T(128)} %adv.1), custom_call_target="tpu_custom_call" | custom-call | flops 1966080000 | bytes 9216000 | tf_op jit(solution)/shard_map/pallas_call | solution.py:615
  99.8 1.5 %copy.10 = f32[8,2560]{1,0:T(8,128)} copy(f32[8,2560]{1,0:T(8,128)} %get-tuple-element.8) | data formatting | bytes 163840
  101.3 3.7 %copy.11 = bf16[1,4800,320]{1,2,0:T(8,128)(2,1)} copy(bf16[1,4800,320]{1,2,0:T(8,128)(2,1)} %bitcast.2) | data formatting | bytes 6144000
